TPU v7x, 32 devices: a whole 2x2x4 slice. The times are simulated.
32 devices in a mesh: groups: 2 (over x), dp: 8 (over z, y), mp: 2 (over core).
Axes of the slice: x: 2, y: 2, z: 4, core: 2. Of those that a mesh axis runs over, the one named last changes fastest.
Arguments:
- frozen_state: bfloat16 [32, 128, 4096], P(('groups', 'dp', 'mp')), parts along dimension 0, may hold values from -6 to 6
- gated_hidden: bfloat16 [32, 128, 14336], P(('groups', 'dp', 'mp')), parts along dimension 0, may hold values from -4 to 4
- lengths: int32 [32], P(('groups', 'dp', 'mp')), parts along dimension 0, may hold values from 1 to 128, as said below
- positives: int32 [32], P('groups'), parts along dimension 0, may hold values from 0 to 15, as said below
- adapter_down_factor: bfloat16 [16, 14336], replicated, may hold values from -0.046875 to 0.046875
- adapter_up_factor: bfloat16 [16, 4096], replicated, may hold values from -1.5 to 1.5
- final_norm_weight: float32 [4096], replicated, may hold values from 0.5 to 1.5
Outputs:
- grad_down: float32 [32, 14336], P('groups', 'mp'), parts along dimension 0
- grad_up: float32 [32, 4096], P('groups', 'mp'), parts along dimension 0
- mean_loss: float32 [2], P('groups'), parts along dimension 0
There are 2 independent parts, one for each index of `groups`. A program takes and returns all parts, laid end to end along the dimension named above; an argument that names none is the same for every part. Nothing has to cross between parts.
Inputs may be any that keep to these rules, and one draw needn't show every extreme that they name: lengths are 1 to 128; passage 0 is unpadded. `positives`: positives_i != i.
All inputs are finite; a program needn't handle non-finite values.
Results may differ from a plain program's by a relative error of at most 0.0045.
Values sent between devices are 32-bit elements; how exact they have to be, the bound alone decides.
A program may use at most 64 MiB of HBM per device.

v0:
```python
import jax
import jax.numpy as jnp
from jax import lax
from jax.sharding import PartitionSpec as P

EPS_NORM = 1e-05
EPS_LEN = 1e-06
TEMP = 0.05
HIGH = lax.Precision.HIGHEST


def softmax_coef(rows_e, row_ids, everyone, targets):
    logits = jnp.dot(rows_e, everyone.T, precision=HIGH) / TEMP
    cols = jnp.arange(everyone.shape[0], dtype=jnp.int32)
    itself = cols[None, :] == row_ids[:, None]
    target = cols[None, :] == targets[:, None]
    lse = jax.nn.logsumexp(jnp.where(itself, -jnp.inf, logits), axis=1)
    loss = lse - jnp.sum(jnp.where(target, logits, 0.0), axis=1)
    prob = jnp.where(itself, 0.0, jnp.exp(logits - lse[:, None]))
    return (prob - target.astype(jnp.float32), loss)


def body(
    frozen_state,
    gated_hidden,
    lengths,
    positives,
    adapter_down_factor,
    adapter_up_factor,
    final_norm_weight,
):
    count, span, width = frozen_state.shape
    lowrank_projection = jnp.einsum(
        "ulw,kw->ulk", gated_hidden, adapter_down_factor, preferred_element_type=jnp.float32
    ).astype(jnp.bfloat16)
    adapted_state = frozen_state.astype(jnp.float32) + jnp.einsum(
        "hui,iw->huw", lowrank_projection, adapter_up_factor, preferred_element_type=jnp.float32
    )
    inverse_norm = lax.rsqrt(
        jnp.mean(adapted_state * adapted_state, axis=-1, keepdims=True) + EPS_NORM
    )
    places = jnp.arange(span, dtype=jnp.int32)
    pooling_weight = jnp.where(places[None, :] < lengths[:, None], 1.0, 0.0).astype(
        jnp.float32
    ) / lengths[:, None].astype(jnp.float32)
    pooled = jnp.einsum(
        "pt,ptd->pd",
        pooling_weight,
        adapted_state * inverse_norm * final_norm_weight,
        precision=HIGH,
    )
    size = jnp.sqrt(jnp.sum(pooled * pooled, axis=-1, keepdims=True) + EPS_LEN)
    embed = pooled / size
    everyone = lax.all_gather(embed, ("dp", "mp"), axis=0, tiled=True)
    total = everyone.shape[0]
    first = lax.axis_index(("dp", "mp")) * count
    own_ids = first + jnp.arange(count, dtype=jnp.int32)
    own_targets = lax.dynamic_slice_in_dim(positives, first, count, 0)
    coef, loss = softmax_coef(embed, own_ids, everyone, own_targets)
    row_part = jnp.dot(coef, everyone, precision=HIGH) / TEMP
    col_terms = jnp.dot(coef.T, embed, precision=HIGH) / TEMP
    d_embed = row_part + lax.psum_scatter(col_terms, ("dp", "mp"), scatter_dimension=0, tiled=True)
    mean_loss = lax.psum(jnp.sum(loss), ("dp", "mp")) / total
    d_pooled = (d_embed - embed * jnp.sum(embed * d_embed, axis=-1, keepdims=True)) / size
    scaled = final_norm_weight * pooling_weight[:, :, None] * d_pooled[:, None, :]
    inner = jnp.sum(adapted_state * scaled, axis=-1, keepdims=True) / width
    state_gradient = (
        inverse_norm * scaled - adapted_state * inverse_norm * inverse_norm * inverse_norm * inner
    ).astype(jnp.bfloat16)
    g_up = jnp.einsum(
        "ptr,ptd->rd", lowrank_projection, state_gradient, preferred_element_type=jnp.float32
    )
    lowrank_gradient = jnp.einsum(
        "seq,iq->sei", state_gradient, adapter_up_factor, preferred_element_type=jnp.float32
    ).astype(jnp.bfloat16)
    g_down = jnp.einsum(
        "ptr,ptf->rf", lowrank_gradient, gated_hidden, preferred_element_type=jnp.float32
    )
    share_down, share_up = (
        lax.psum_scatter(g_down, "mp", scatter_dimension=1, tiled=True),
        lax.psum_scatter(g_up, "mp", scatter_dimension=1, tiled=True),
    )
    grad_down, grad_up = lax.psum((share_down, share_up), "dp")
    return (grad_down, grad_up, jnp.reshape(mean_loss, (1,)))


def solution(mesh):
    in_specs = (
        P(("groups", "dp", "mp"), None, None),
        P(("groups", "dp", "mp"), None, None),
        P(("groups", "dp", "mp")),
        P("groups"),
        P(),
        P(),
        P(),
    )
    out_specs = (P("groups", "mp"), P("groups", "mp"), P("groups"))
    return jax.shard_map(body, mesh=mesh, in_specs=in_specs, out_specs=out_specs, check_vma=False)
```

profile of v0, /device:TPU:0, one launch (start us, length us, event | category | flops | bytes accessed | tf_op | source)
XLA Modules:
  0.0 247.4 jit_solution(6587733674038308639)
XLA Ops:
  7.2 0.0 copy-start
  7.2 0.0 copy-start.3
  7.2 0.0 all-reduce.5.cloned.1.call-start
  7.2 0.0 copy-start.2
  8.0 0.2 copy-done
  8.2 3.1 %fusion.9 = bf16[128,16]{0,1:T(8,128)(2,1)S(1)} fusion(bf16[16,14336]{1,0:T(8,128)(2,1)S(1)} %copy-done, bf16[1,128,14336]{2,1,0:T(8,128)(2,1)} %param.8), kind=kOutput, calls=%fused_computation.15 | convolution fusion | flops 58722304 | bytes 4132864 | tf_op jit(solution)/shard_map/ulw,kw->ulk/dot_general | solution.py:33
  11.3 0.0 copy-done.3
  11.3 0.0 copy-done.2
  11.3 0.0 copy-start.4
  11.3 0.5 multiply_reduce_fusion.1
  11.8 0.0 copy-start.5
  11.9 0.0 copy-start.6
  11.9 0.1 copy-done.4
  12.0 1.3 fusion.5
  13.3 0.6 multiply_reduce_fusion.3
  14.6 23.8 %all-gather = f32[65536]{0:T(1024)S(1)} all-gather(f32[4096]{0:T(1024)S(1)} %broadcast_divide_fusion), channel_id=2, replica_groups=mesh['groups'=2,'dp'=8,'mp'=2] {'dp','mp'}, dimensions={0}, use_global_device_ids=true | all-gather | bytes 278528 | tf_op jit(solution)/shard_map/all_gather | solution.py:54
  38.4 0.1 reshape.322
  38.5 1.0 fusion.31
  40.2 0.0 copy-done.5
  40.2 0.7 dynamic_slice.3
  41.5 1.3 fusion.17
  43.4 0.7 fusion.16
  44.1 0.8 multiply_multiply_fusion.1
  44.9 0.0 all-reduce.5.cloned.1.call-update
  44.9 0.0 reduce-scatter.5.cloned.1.call-start
  45.0 0.3 fusion.22
  45.2 0.0 copy-done.6
  45.3 0.6 dynamic-slice
  45.9 85.3 %all-reduce.5.cloned.1.call-done = f32[16,4096]{1,0:T(8,128)} async-done(((f32[16,4096]{1,0:T(8,128)}), f32[16,4096]{1,0:T(8,128)}) %all-reduce.5.cloned.1.call-update) | async-done | bytes 262160
  131.2 2.2 multiply_reduce_fusion.2
  133.3 0.6 broadcast_multiply_fusion
  134.0 1.6 subtract_divide_fusion
  135.5 0.5 multiply_reduce_fusion
  136.0 0.7 fusion.13
  136.7 1.0 copy-done.1
  137.7 1.0 fusion.32
  138.7 0.0 reduce-scatter.5.cloned.1.call-update
  138.7 0.0 reduce-scatter.3.cloned.1.call-start
  138.7 4.9 %fusion.1 = f32[16,14336]{1,0:T(8,128)} fusion(bf16[1,128,14336]{2,1,0:T(8,128)(2,1)} %param.8, bf16[128,4096]{1,0:T(8,128)(2,1)} %copy-done.1, bf16[16,4096]{1,0:T(8,128)(2,1)S(1)} %copy-done.3), kind=kOutput, calls=%fused_computation.2 | convolution fusion | flops 75499520 | bytes 5767168 | tf_op jit(solution)/shard_map/ptr,ptf->rf/dot_general | solution.py:76
  143.6 0.0 reduce-scatter.3.cloned.1.call-update
  143.6 0.0 all-reduce.7.cloned.1.call-start
  143.7 3.3 %reduce-scatter.5.cloned.1.call-done = f32[16,2048]{1,0:T(8,128)} async-done(((f32[16,4096]{1,0:T(8,128)}), f32[16,2048]{1,0:T(8,128)}) %reduce-scatter.5.cloned.1.call-update) | async-done | bytes 131088 | tf_op jit(solution)/shard_map/reduce_scatter | solution.py:81
  147.0 12.0 %reduce-scatter.3.cloned.1.call-done = f32[16,7168]{1,0:T(8,128)} async-done(((f32[16,14336]{1,0:T(8,128)}), f32[16,7168]{1,0:T(8,128)}) %reduce-scatter.3.cloned.1.call-update) | async-done | bytes 458768 | tf_op jit(solution)/shard_map/reduce_scatter | solution.py:80
  159.0 0.0 all-reduce.7.cloned.1.call-update
  159.6 35.3 %psum.23 = f32[]{:T(128)} all-reduce(f32[]{:T(128)} %bitcast.23), channel_id=1, replica_groups=mesh['groups'=2,'dp'=8,'mp'=2] {'dp','mp'}, use_global_device_ids=true, to_apply=%region_12.13 | all-reduce | flops 1 | bytes 8 | tf_op jit(solution)/shard_map/psum | solution.py:63
  195.5 40.8 %all-reduce.7.cloned.1.call-done = (f32[16,7168]{1,0:T(8,128)}, f32[16,2048]{1,0:T(8,128)}) async-done(((f32[16,7168]{1,0:T(8,128)}, f32[16,2048]{1,0:T(8,128)}), (f32[16,7168]{1,0:T(8,128)}, f32[16,2048]{1,0:T(8,128)})) %all-reduce.7.cloned.1.call-update) | async-done | bytes 589840 | tf_op jit(solution)/shard_map/psum | solution.py:83
  236.3 1.8 copy.14
  238.1 1.6 copy.15
  (6 shorter events, 0.0 us)
Async XLA Ops:
  7.2 1.0 copy-start
  7.2 4.1 %copy-start.3 = (bf16[16,4096]{1,0:T(8,128)(2,1)S(1)}, bf16[16,4096]{1,0:T(8,128)(2,1)}, u32[]{:S(2)}) copy-start(bf16[16,4096]{1,0:T(8,128)(2,1)} %param.12) | copy-start | bytes 393220
  7.2 124.0 %all-reduce.5.cloned.1.call-start = ((), (), s32[]{:S(2)}) async-start(), calls=%async_computation.4 | async-start | bytes 524288
  7.2 4.0 %copy-start.2 = (bf16[1,128,4096]{2,1,0:T(8,128)(2,1)S(1)}, bf16[1,128,4096]{2,1,0:T(8,128)(2,1)}, u32[]{:S(2)}) copy-start(bf16[1,128,4096]{2,1,0:T(8,128)(2,1)} %param.7) | copy-start | bytes 3145732
  11.3 0.7 copy-start.4
  11.8 28.3 %copy-start.5 = (s32[16]{0:T(128)S(1)}, s32[16]{0:T(128)}, u32[]{:S(2)}) copy-start(s32[16]{0:T(128)} %param.10) | copy-start | bytes 196
  11.9 33.4 %copy-start.6 = (u32[32]{0:T(128)S(1)}, u32[32]{0:T(128)}, u32[]{:S(2)}) copy-start(u32[32]{0:T(128)} %constant.47) | copy-start | bytes 388
  44.9 102.1 %reduce-scatter.5.cloned.1.call-start = ((), (), s32[]{:S(2)}) async-start(), calls=%async_computation.3 | async-start | bytes 393216 | tf_op jit(solution)/shard_map/reduce_scatter | solution.py:81
  136.7 1.0 copy-start.1
  138.7 20.3 %reduce-scatter.3.cloned.1.call-start = ((), (), s32[]{:S(2)}) async-start(), calls=%async_computation.2 | async-start | bytes 1376256 | tf_op jit(solution)/shard_map/reduce_scatter | solution.py:80
  143.6 92.7 %all-reduce.7.cloned.1.call-start = ((), (), s32[]{:S(2)}) async-start(), calls=%async_computation.5 | async-start | bytes 1179648 | tf_op jit(solution)/shard_map/psum | solution.py:83
Sparse Core Ops, SparseCore 0:
  45.0 86.0 all-reduce.4
  138.8 8.1 reduce-scatter.4
  149.3 9.5 reduce-scatter.2
  162.2 74.0 all-reduce.6
where the time goes:
time: 248 us; the launch traced here: 247 us
  waiting for transfers between devices  141 us (57%)
  blocking collectives  59.1 us (24%)
  between operations  19.7 us (8%)
  matrix products  12 us (5%)
  other arithmetic  8.94 us (4%)
  local copies, waits for them, and re-layouts  6.09 us (2%)
    unnamed x5, waiting for transfers between devices  85.3 us
    psum x1, waiting for transfers between devices, body(): grad_down, grad_up = lax.psum((share_down, share_up), 'dp')  40.8 us
    psum x1, blocking collectives, body(): mean_loss = lax.psum(jnp.sum(loss), ('dp', 'mp')) / total  35.3 us
    all_gather x1, blocking collectives, body(): everyone = lax.all_gather(embed, ('dp', 'mp'), axis=0, tiled=True)  23.8 us
    reduce_scatter x1, waiting for transfers between devices, body(): lax.psum_scatter(g_down, 'mp', scatter_dimension=1, tiled=True)  12 us
    unnamed x17, local copies, waits for them, and re-layouts  5.37 us
  transfers between devices with their start and end apart: 4, of which 4 were waited for; matrix products, arithmetic and copies ran while one was open for 2% of the time, Pallas kernels for 0%

commit v1 on v0

v1 whole, which is shorter than its diff:
```python
import functools
import math

import jax
import jax.numpy as jnp
from jax import lax
from jax.experimental import pallas as pl
from jax.experimental.pallas import tpu as pltpu
from jax.sharding import PartitionSpec as P

EPS_NORM = 1e-05
EPS_LEN = 1e-06
TEMP = 0.05
LANE = 128
MESH = pl.DeviceIdType.MESH
F32 = jnp.float32
BF16 = jnp.bfloat16


def plan(n, width, hidden):
    blocks = (width + hidden) // 2 // LANE
    pieces = 3 if blocks % (3 * n) == 0 else 1
    unit = n * pieces
    padded = (blocks + unit - 1) // unit * unit
    ny = max(d for d in range(1, int(math.isqrt(n)) + 1) if n % d == 0)
    return pieces, padded * LANE, ny, n // ny


def nt_dot(a, b, precision=None):
    return lax.dot_general(
        a, b, (((1,), (1,)), ((), ())), preferred_element_type=F32, precision=precision
    )


def kernel(
    n,
    hidden_chunks,
    frozen_hbm,
    hidden_hbm,
    lengths_ref,
    positives_ref,
    down_hbm,
    up_ref,
    gain_ref,
    gdown_ref,
    gup_ref,
    loss_ref,
    frozen,
    hidden,
    down,
    state,
    own,
    land,
    both,
    sib,
    ybuf,
    zbuf,
    res,
    load_sem,
    esend,
    erecv,
    fsend,
    frecv,
    ssend,
    srecv,
    ysend,
    yrecv,
    zsend,
    zrecv,
    azsend,
    azrecv,
    aysend,
    ayrecv,
):
    span, width = frozen.shape
    units = hidden.shape[1]
    rank = up_ref.shape[0]
    total = 2 * n
    rows = width // LANE
    pieces, cols, ny, nz = plan(n, width, units)
    pw = cols // pieces
    yw = pw // ny
    zw = yw // nz
    hu, hd = width // 2, units // 2
    dp = lax.axis_index("dp")
    mp = lax.axis_index("mp")
    other = 1 - mp
    me = dp * 2 + mp
    y = lax.rem(dp, ny)
    z = lax.div(dp, ny)

    cw = units // hidden_chunks
    loads = []
    for c in range(hidden_chunks):
        at = pl.ds(c * cw, cw)
        loads.append(
            (
                pltpu.make_async_copy(down_hbm.at[:, at], down.at[:, at], load_sem.at[1, c]),
                pltpu.make_async_copy(
                    hidden_hbm.at[0, :, at], hidden.at[:, at], load_sem.at[0, c]
                ),
            )
        )
    frozen_load = pltpu.make_async_copy(
        frozen_hbm.at[0], frozen, load_sem.at[0, hidden_chunks]
    )
    for pair in loads:
        for copy in pair:
            copy.start()
    frozen_load.start()

    barrier = pltpu.get_barrier_semaphore()

    def greet(k, _):
        pl.semaphore_signal(
            barrier, inc=1, device_id={"dp": lax.rem(dp + k, n)}, device_id_type=MESH
        )
        return 0

    lax.fori_loop(1, n, greet, 0)
    pl.semaphore_signal(barrier, inc=1, device_id={"mp": other}, device_id_type=MESH)

    low = jnp.zeros((span, rank), F32)
    for c in range(hidden_chunks):
        for copy in loads[c]:
            copy.wait()
        at = pl.ds(c * cw, cw)
        low = low + nt_dot(hidden[:, at], down[:, at])
    low = low.astype(BF16)
    low_t = low.astype(F32).T.astype(BF16)
    frozen_load.wait()

    tile = 512
    square = jnp.zeros((span, LANE), F32)
    for c in range(width // tile):
        at = pl.ds(c * tile, tile)
        s = frozen[:, at].astype(F32) + jnp.dot(
            low, up_ref[:, at], preferred_element_type=F32
        )
        state[:, at] = s
        for g in range(tile // LANE):
            part = s[:, g * LANE : (g + 1) * LANE]
            square = square + part * part
    inv = lax.rsqrt(jnp.sum(square, axis=1, keepdims=True) / width + EPS_NORM)
    length = lengths_ref[0]
    places = lax.broadcasted_iota(jnp.int32, (span, 1), 0)
    weight = jnp.where(places < length, 1.0, 0.0).astype(F32) / length.astype(F32)
    wi = weight * inv
    for r in range(rows):
        at = pl.ds(r * LANE, LANE)
        own[pl.ds(r, 1), :] = (
            jnp.sum(state[:, at] * wi, axis=0, keepdims=True) * gain_ref[:, at]
        )

    pl.semaphore_wait(barrier, n)

    def row(i):
        return pl.ds(pl.multiple_of(i * rows, rows), rows)

    def share(k):
        return pltpu.make_async_remote_copy(
            src_ref=own,
            dst_ref=land.at[row(me)],
            send_sem=esend.at[k],
            recv_sem=erecv.at[k],
            device_id={"dp": lax.rem(dp + k, n)},
            device_id_type=MESH,
        )

    def forward(k):
        peer = lax.rem(dp + n - k, n) * 2 + mp
        return pltpu.make_async_remote_copy(
            src_ref=land.at[row(peer)],
            dst_ref=land.at[row(peer)],
            send_sem=fsend.at[k],
            recv_sem=frecv.at[k],
            device_id={"mp": other},
            device_id_type=MESH,
        )

    def start_share(k, _):
        share(k).start()
        return 0

    lax.fori_loop(1, n, start_share, 0)
    land[row(me), :] = own[...]
    forward(0).start()

    def pass_on(k, _):
        share(k).wait_recv()
        forward(k).start()
        return 0

    lax.fori_loop(1, n, pass_on, 0)

    def arrive(k, _):
        forward(k).wait()
        return 0

    lax.fori_loop(0, n, arrive, 0)

    def sent(k, _):
        share(k).wait_send()
        return 0

    lax.fori_loop(1, n, sent, 0)

    ri = lax.broadcasted_iota(jnp.int32, (total, total), 0)
    ci = lax.broadcasted_iota(jnp.int32, (total, total), 1)
    eye = ri == ci
    if total <= 16:
        sums = [jnp.zeros((total, LANE), F32) for _ in range(total)]
        for r in range(rows):
            a = land[pl.ds(r, total, stride=rows), :]
            for j in range(total):
                sums[j] = sums[j] + a * a[j : j + 1, :]
        gram = jnp.zeros((total, total), F32)
        for j in range(total):
            gram = jnp.where(ci == j, jnp.sum(sums[j], axis=1, keepdims=True), gram)
    else:
        gram = jnp.zeros((total, total), F32)
        for r in range(rows):
            a = land[pl.ds(r, total, stride=rows), :]
            gram = gram + nt_dot(a, a, lax.Precision.HIGHEST)
    diag = jnp.where(eye, gram, 0.0)
    size_col = jnp.sqrt(jnp.sum(diag, axis=1, keepdims=True) + EPS_LEN)
    size_row = jnp.sqrt(jnp.sum(diag, axis=0, keepdims=True) + EPS_LEN)
    cosine = gram / size_col / size_row
    logits = cosine / TEMP
    masked = jnp.where(eye, -jnp.inf, logits)
    top = jnp.max(masked, axis=0, keepdims=True)
    lse = top + jnp.log(jnp.sum(jnp.exp(masked - top), axis=0, keepdims=True))
    target = ri == positives_ref[...]
    loss = lse - jnp.sum(jnp.where(target, logits, 0.0), axis=0, keepdims=True)
    loss_ref[0] = jnp.sum(loss) / total
    coef_t = jnp.where(eye, 0.0, jnp.exp(logits - lse)) - jnp.where(target, 1.0, 0.0)
    mine_row = jnp.sum(jnp.where(ri == me, coef_t, 0.0), axis=0, keepdims=True)
    picked = jnp.where(ci == me, coef_t, 0.0) + jnp.where(eye, mine_row, 0.0)
    m = jnp.sum(picked, axis=1, keepdims=True) / TEMP
    cos_me = jnp.sum(jnp.where(ci == me, cosine, 0.0), axis=1, keepdims=True)
    along = jnp.sum(m * cos_me, axis=0, keepdims=True)
    is_me = ri[:, 0:1] == me
    size_me = jnp.sum(jnp.where(is_me, size_col, 0.0), axis=0, keepdims=True)
    q = (m - jnp.where(is_me, along, 0.0)) / size_col / size_me

    scaled = []
    inner = jnp.zeros((span, LANE), F32)
    for r in range(rows):
        at = pl.ds(r * LANE, LANE)
        a = land[pl.ds(r, total, stride=rows), :]
        sc = jnp.sum(a * q, axis=0, keepdims=True) * gain_ref[:, at]
        scaled.append(sc)
        inner = inner + state[:, at] * sc
    inner = jnp.sum(inner, axis=1, keepdims=True) * weight / width
    back = inv * inv * inv * inner
    dlow = jnp.zeros((span, rank), F32)
    per = tile // LANE
    for c in range(width // tile):
        at = pl.ds(c * tile, tile)
        sc = jnp.concatenate(scaled[c * per : (c + 1) * per], axis=1)
        ds = (wi * sc - state[:, at] * back).astype(BF16)
        dlow = dlow + nt_dot(ds, up_ref[:, at])
        half, col = divmod(c * tile, hu)
        both[half, :, pl.ds(col, tile)] = jnp.dot(low_t, ds, preferred_element_type=F32)
    dlow_t = dlow.astype(BF16).astype(F32).T.astype(BF16)

    def compute_piece(p, half):
        lo, hi = max(p * pw, hu), min((p + 1) * pw, hu + hd)
        while lo < hi:
            w = min(1024, hi - lo)
            at = pl.ds(pl.multiple_of(half * hd + (lo - hu), LANE), w)
            both[half, :, pl.ds(lo, w)] = jnp.dot(
                dlow_t, hidden[:, at], preferred_element_type=F32
            )
            lo += w
        lo = max(p * pw, hu + hd)
        if lo < (p + 1) * pw:
            both[half, :, pl.ds(lo, (p + 1) * pw - lo)] = jnp.zeros(
                (rank, (p + 1) * pw - lo), F32
            )

    waits = []

    def to_sibling(p):
        at = pl.ds(p * pw, pw)
        return pltpu.make_async_remote_copy(
            src_ref=both.at[other, :, at],
            dst_ref=sib.at[:, at],
            send_sem=ssend.at[p],
            recv_sem=srecv.at[p],
            device_id={"mp": other},
            device_id_type=MESH,
        )

    def chunk(base, size, index):
        return pl.ds(pl.multiple_of(base + index * size, LANE), size)

    def along_y(p, k):
        to = lax.rem(y + k, ny)
        return pltpu.make_async_remote_copy(
            src_ref=both.at[mp, :, chunk(p * pw, yw, to)],
            dst_ref=ybuf.at[p, k - 1],
            send_sem=ysend.at[p, k - 1],
            recv_sem=yrecv.at[p, k - 1],
            device_id={"dp": z * ny + to},
            device_id_type=MESH,
        )

    def along_z(p, k):
        to = lax.rem(z + k, nz)
        return pltpu.make_async_remote_copy(
            src_ref=both.at[mp, :, chunk(p * pw + y * yw, zw, to)],
            dst_ref=zbuf.at[p, k - 1],
            send_sem=zsend.at[p, k - 1],
            recv_sem=zrecv.at[p, k - 1],
            device_id={"dp": to * ny + y},
            device_id_type=MESH,
        )

    def gather_z(p, k):
        to = lax.rem(z + k, nz)
        at = chunk(p * pw + y * yw, zw, z)
        return pltpu.make_async_remote_copy(
            src_ref=res.at[:, at],
            dst_ref=res.at[:, at],
            send_sem=azsend.at[p, k - 1],
            recv_sem=azrecv.at[p, k - 1],
            device_id={"dp": to * ny + y},
            device_id_type=MESH,
        )

    def gather_y(p, k):
        to = lax.rem(y + k, ny)
        at = chunk(p * pw, yw, y)
        return pltpu.make_async_remote_copy(
            src_ref=res.at[:, at],
            dst_ref=res.at[:, at],
            send_sem=aysend.at[p, k - 1],
            recv_sem=ayrecv.at[p, k - 1],
            device_id={"dp": z * ny + to},
            device_id_type=MESH,
        )

    def start(copy):
        copy.start()
        waits.append(copy)

    for p in range(pieces):
        compute_piece(p, other)
        start(to_sibling(p))
    for p in range(pieces):
        compute_piece(p, mp)
        to_sibling(p).wait_recv()
        at = pl.ds(p * pw, pw)
        both[mp, :, at] = both[mp, :, at] + sib[:, at]
        for k in range(1, ny):
            start(along_y(p, k))
    for p in range(pieces):
        at = chunk(p * pw, yw, y)
        acc = both[mp, :, at]
        for k in range(1, ny):
            along_y(p, k).wait_recv()
            acc = acc + ybuf[p, k - 1]
        both[mp, :, at] = acc
        for k in range(1, nz):
            start(along_z(p, k))
    for p in range(pieces):
        at = chunk(p * pw + y * yw, zw, z)
        acc = both[mp, :, at]
        for k in range(1, nz):
            along_z(p, k).wait_recv()
            acc = acc + zbuf[p, k - 1]
        res[:, at] = acc
        for k in range(1, nz):
            start(gather_z(p, k))
    for p in range(pieces):
        for k in range(1, nz):
            gather_z(p, k).wait_recv()
        for k in range(1, ny):
            start(gather_y(p, k))
    for p in range(pieces):
        for k in range(1, ny):
            gather_y(p, k).wait_recv()
        lo, hi = p * pw, min((p + 1) * pw, hu)
        if lo < hi:
            gup_ref[:, pl.ds(lo, hi - lo)] = res[:, pl.ds(lo, hi - lo)]
        lo, hi = max(p * pw, hu), min((p + 1) * pw, hu + hd)
        if lo < hi:
            gdown_ref[:, pl.ds(lo - hu, hi - lo)] = res[:, pl.ds(lo, hi - lo)]
    for copy in waits:
        copy.wait_send()


def body(
    frozen_state,
    gated_hidden,
    lengths,
    positives,
    adapter_down_factor,
    adapter_up_factor,
    final_norm_weight,
    *,
    n,
):
    _, span, width = frozen_state.shape
    units = gated_hidden.shape[2]
    rank = adapter_down_factor.shape[0]
    total = positives.shape[0]
    pieces, cols, ny, nz = plan(n, width, units)
    yw = cols // pieces // ny
    zw = yw // nz
    chunks = 7
    sy, sz = max(ny - 1, 1), max(nz - 1, 1)
    dma = pltpu.SemaphoreType.DMA
    vmem = pl.BlockSpec(memory_space=pltpu.VMEM)
    smem = pl.BlockSpec(memory_space=pltpu.SMEM)
    hbm = pl.BlockSpec(memory_space=pl.ANY)
    grad_down, grad_up, mean_loss = pl.pallas_call(
        functools.partial(kernel, n, chunks),
        out_shape=(
            jax.ShapeDtypeStruct((rank, units // 2), F32),
            jax.ShapeDtypeStruct((rank, width // 2), F32),
            jax.ShapeDtypeStruct((1,), F32),
        ),
        in_specs=[hbm, hbm, smem, vmem, hbm, vmem, vmem],
        out_specs=(vmem, vmem, smem),
        scratch_shapes=[
            pltpu.VMEM((span, width), BF16),
            pltpu.VMEM((span, units), BF16),
            pltpu.VMEM((rank, units), BF16),
            pltpu.VMEM((span, width), F32),
            pltpu.VMEM((width // LANE, LANE), F32),
            pltpu.VMEM((total * (width // LANE), LANE), F32),
            pltpu.VMEM((2, rank, cols), F32),
            pltpu.VMEM((rank, cols), F32),
            pltpu.VMEM((pieces, sy, rank, yw), F32),
            pltpu.VMEM((pieces, sz, rank, zw), F32),
            pltpu.VMEM((rank, cols), F32),
            dma((2, chunks + 1)),
            dma((n,)),
            dma((n,)),
            dma((n,)),
            dma((n,)),
            dma((pieces,)),
            dma((pieces,)),
            dma((pieces, sy)),
            dma((pieces, sy)),
            dma((pieces, sz)),
            dma((pieces, sz)),
            dma((pieces, sz)),
            dma((pieces, sz)),
            dma((pieces, sy)),
            dma((pieces, sy)),
        ],
        compiler_params=pltpu.CompilerParams(
            collective_id=0, has_side_effects=True, vmem_limit_bytes=40 * 2**20
        ),
    )(
        frozen_state,
        gated_hidden,
        lengths,
        positives.reshape(1, total),
        adapter_down_factor,
        adapter_up_factor,
        final_norm_weight.reshape(1, width),
    )
    return grad_down, grad_up, mean_loss


def solution(mesh):
    in_specs = (
        P(("groups", "dp", "mp"), None, None),
        P(("groups", "dp", "mp"), None, None),
        P(("groups", "dp", "mp")),
        P("groups"),
        P(),
        P(),
        P(),
    )
    out_specs = (P("groups", "mp"), P("groups", "mp"), P("groups"))
    return jax.shard_map(
        functools.partial(body, n=mesh.shape["dp"]),
        mesh=mesh,
        in_specs=in_specs,
        out_specs=out_specs,
        check_vma=False,
    )
```

time: 248 us -> 52.9 us (0.21)
  waiting for transfers between devices: 141 us -> 0 us
  blocking collectives: 59.1 us -> 0 us
  Pallas kernels: 0 us -> 41.4 us
  between operations: 19.7 us -> 3.12 us
  matrix products: 12 us -> 0 us
  other arithmetic: 8.94 us -> 0 us
    unnamed x5 -> x0, waiting for transfers between devices: 85.3 us -> none
    pallas_call x0 -> x1, Pallas kernels: none -> 41.4 us  [body(): pl.pallas_call(functools.partial(kernel, n, chunks), out_shape=(jax.Shape...]
    psum x1 -> x0, waiting for transfers between devices: 40.8 us -> none  [body(): grad_down, grad_up = lax.psum((share_down, share_up), 'dp')]
    psum x1 -> x0, blocking collectives: 35.3 us -> none  [body(): mean_loss = lax.psum(jnp.sum(loss), ('dp', 'mp')) / total]
    all_gather x1 -> x0, blocking collectives: 23.8 us -> none  [body(): everyone = lax.all_gather(embed, ('dp', 'mp'), axis=0, tiled=True)]
    reduce_scatter x2 -> x0, waiting for transfers between devices: 15.3 us -> none  [the longest x1 12 us: body(): lax.psum_scatter(g_down, 'mp', scatter_dimension=1, tiled=True)]
    dot_general x7 -> x0, matrix products: 12 us -> none  [the longest x1 4.87 us: body(): jnp.einsum('ptr,ptf->rf', lowrank_gradient, gated_hidden, preferred_eleme...]
    reduce_sum x4 -> x0, other arithmetic: 4.53 us -> none  [the longest x1 2.17 us: body(): jnp.sum(embed * d_embed, axis=-1, keepdims=True)]
  transfers between devices with their start and end apart: 4 -> 0, of which waited for: 4 -> 0; matrix products, arithmetic and copies ran while one was open for 2% -> 0% of each run, Pallas kernels for 0% -> 0%
where the time goes in v1:
time: 52.9 us; the launch traced here: 52.5 us
  Pallas kernels  41.4 us (78%)
  local copies, waits for them, and re-layouts  7.97 us (15%)
  between operations  3.12 us (6%)
    pallas_call x1, Pallas kernels, body(): pl.pallas_call(functools.partial(kernel, n, chunks), out_shape=(jax.Shape...  41.4 us
    unnamed x14, local copies, waits for them, and re-layouts  7.97 us

profile of v1, /device:TPU:0, one launch (start us, length us, event | category | flops | bytes accessed | tf_op | source)
XLA Modules:
  0.0 52.5 jit_solution(480586195461711309)
XLA Ops:
  1.3 0.0 copy-start
  1.3 2.0 %copy-done = bf16[1,128,14336]{2,1,0:T(8,128)(2,1)S(1)} copy-done((bf16[1,128,14336]{2,1,0:T(8,128)(2,1)S(1)}, bf16[1,128,14336]{2,1,0:T(8,128)(2,1)}, u32[]{:S(2)}) %copy-start) | copy-done | bytes 3670040
  3.3 0.0 copy-start.1
  3.3 1.2 %copy-done.1 = bf16[1,128,4096]{2,1,0:T(8,128)(2,1)S(1)} copy-done((bf16[1,128,4096]{2,1,0:T(8,128)(2,1)S(1)}, bf16[1,128,4096]{2,1,0:T(8,128)(2,1)}, u32[]{:S(2)}) %copy-start.1) | copy-done | bytes 1048600
  4.5 0.0 copy-start.2
  4.5 1.0 %copy-done.2 = bf16[16,14336]{1,0:T(8,128)(2,1)S(1)} copy-done((bf16[16,14336]{1,0:T(8,128)(2,1)S(1)}, bf16[16,14336]{1,0:T(8,128)(2,1)}, u32[]{:S(2)}) %copy-start.2) | copy-done | bytes 458776
  5.6 0.0 copy-start.3
  5.6 0.9 %copy-done.3 = bf16[16,4096]{1,0:T(8,128)(2,1)S(1)} copy-done((bf16[16,4096]{1,0:T(8,128)(2,1)S(1)}, bf16[16,4096]{1,0:T(8,128)(2,1)}, u32[]{:S(2)}) %copy-start.3) | copy-done | bytes 131096
  6.5 0.0 copy-start.4
  6.5 0.7 %copy-done.4 = f32[4096]{0:T(1024)S(1)} copy-done((f32[4096]{0:T(1024)S(1)}, f32[4096]{0:T(1024)}, u32[]{:S(2)}) %copy-start.4) | copy-done | bytes 16408
  7.2 0.0 copy-start.5
  7.2 0.7 %copy-done.5 = s32[16]{0:T(128)S(1)} copy-done((s32[16]{0:T(128)S(1)}, s32[16]{0:T(128)}, u32[]{:S(2)}) %copy-start.5) | copy-done | bytes 88
  7.8 41.4 %shard_map.94 = (f32[16,7168]{1,0:T(8,128)S(1)}, f32[16,2048]{1,0:T(8,128)S(1)}, f32[1]{0:T(128)}) custom-call(bf16[1,128,4096]{2,1,0:T(8,128)(2,1)S(1)} %copy-done.1, bf16[1,128,14336]{2,1,0:T(8,128)(2,1)S(1)} %copy-done, s32[1]{0:T(128)S(6)} %copy.13.lengths_ref, s32[1,16]{1,0:T(1,128)S(1)} %bitcast.3, bf16[16,14336]{1,0:T(8,128)(2,1)S(1)} %copy-done.2, ...), custom_call_target="tpu_custom_call" | custom-call | tf_op jit(solution)/shard_map/pallas_call | solution.py:418
  49.3 0.8 %copy.14 = f32[16,7168]{1,0:T(8,128)} copy(f32[16,7168]{1,0:T(8,128)S(1)} %get-tuple-element.6) | data formatting | bytes 917504
  50.1 0.7 %copy.15 = f32[16,2048]{1,0:T(8,128)} copy(f32[16,2048]{1,0:T(8,128)S(1)} %get-tuple-element.7) | data formatting | bytes 262144
Async XLA Ops:
  1.3 2.0 %copy-start = (bf16[1,128,14336]{2,1,0:T(8,128)(2,1)S(1)}, bf16[1,128,14336]{2,1,0:T(8,128)(2,1)}, u32[]{:S(2)}) copy-start(bf16[1,128,14336]{2,1,0:T(8,128)(2,1)} %hidden_hbm.1) | copy-start | bytes 11010052
  3.3 1.2 %copy-start.1 = (bf16[1,128,4096]{2,1,0:T(8,128)(2,1)S(1)}, bf16[1,128,4096]{2,1,0:T(8,128)(2,1)}, u32[]{:S(2)}) copy-start(bf16[1,128,4096]{2,1,0:T(8,128)(2,1)} %frozen_hbm.1) | copy-start | bytes 3145732
  4.5 1.0 %copy-start.2 = (bf16[16,14336]{1,0:T(8,128)(2,1)S(1)}, bf16[16,14336]{1,0:T(8,128)(2,1)}, u32[]{:S(2)}) copy-start(bf16[16,14336]{1,0:T(8,128)(2,1)} %down_hbm.1) | copy-start | bytes 1376260
  5.6 0.9 %copy-start.3 = (bf16[16,4096]{1,0:T(8,128)(2,1)S(1)}, bf16[16,4096]{1,0:T(8,128)(2,1)}, u32[]{:S(2)}) copy-start(bf16[16,4096]{1,0:T(8,128)(2,1)} %up_ref.1) | copy-start | bytes 393220
  6.5 0.7 %copy-start.4 = (f32[4096]{0:T(1024)S(1)}, f32[4096]{0:T(1024)}, u32[]{:S(2)}) copy-start(f32[4096]{0:T(1024)} %param.13) | copy-start | bytes 49156
  7.2 0.7 %copy-start.5 = (s32[16]{0:T(128)S(1)}, s32[16]{0:T(128)}, u32[]{:S(2)}) copy-start(s32[16]{0:T(128)} %param.10) | copy-start | bytes 196

commit v2 on v1

--- a/solution.py
+++ b/solution.py
@@ -37,24 +37,27 @@
     hidden_chunks,
     frozen_hbm,
     hidden_hbm,
-    lengths_ref,
-    positives_ref,
+    lengths_hbm,
+    positives_hbm,
     down_hbm,
-    up_ref,
-    gain_ref,
+    up_hbm,
+    gain_hbm,
     gdown_ref,
     gup_ref,
     loss_ref,
     frozen,
     hidden,
     down,
+    lengths_ref,
+    positives_ref,
+    up_ref,
+    gain_ref,
     state,
     own,
     land,
     both,
     sib,
-    ybuf,
-    zbuf,
+    slots,
     res,
     load_sem,
     esend,
@@ -63,14 +66,10 @@
     frecv,
     ssend,
     srecv,
-    ysend,
-    yrecv,
-    zsend,
-    zrecv,
-    azsend,
-    azrecv,
-    aysend,
-    ayrecv,
+    rsend,
+    rrecv,
+    gsend,
+    grecv,
 ):
     span, width = frozen.shape
     units = hidden.shape[1]
@@ -79,8 +78,7 @@
     rows = width // LANE
     pieces, cols, ny, nz = plan(n, width, units)
     pw = cols // pieces
-    yw = pw // ny
-    zw = yw // nz
+    first_z = 1 if pieces > 1 else 0
     hu, hd = width // 2, units // 2
     dp = lax.axis_index("dp")
     mp = lax.axis_index("mp")
@@ -101,13 +99,23 @@
                 ),
             )
         )
-    frozen_load = pltpu.make_async_copy(
-        frozen_hbm.at[0], frozen, load_sem.at[0, hidden_chunks]
-    )
+    later = [
+        pltpu.make_async_copy(src, dst, load_sem.at[2, i])
+        for i, (src, dst) in enumerate(
+            (
+                (up_hbm, up_ref),
+                (frozen_hbm.at[0], frozen),
+                (gain_hbm, gain_ref),
+                (lengths_hbm, lengths_ref),
+                (positives_hbm, positives_ref),
+            )
+        )
+    ]
     for pair in loads:
         for copy in pair:
             copy.start()
-    frozen_load.start()
+    for copy in later:
+        copy.start()
 
     barrier = pltpu.get_barrier_semaphore()
 
@@ -128,7 +136,8 @@
         low = low + nt_dot(hidden[:, at], down[:, at])
     low = low.astype(BF16)
     low_t = low.astype(F32).T.astype(BF16)
-    frozen_load.wait()
+    for copy in later:
+        copy.wait()
 
     tile = 512
     square = jnp.zeros((span, LANE), F32)
@@ -281,6 +290,10 @@
 
     waits = []
 
+    def start(copy):
+        copy.start()
+        waits.append(copy)
+
     def to_sibling(p):
         at = pl.ds(p * pw, pw)
         return pltpu.make_async_remote_copy(
@@ -292,58 +305,62 @@
             device_id_type=MESH,
         )
 
+    along_y = (ny, y, lambda to: z * ny + to)
+    along_z = (nz, z, lambda to: to * ny + y)
+
+    def axes(p):
+        return (along_z, along_y) if p < first_z else (along_y, along_z)
+
+    def span_of(p, level):
+        base, size = p * pw, pw
+        for places, place, _ in axes(p)[:level]:
+            size = size // places
+            base = base + place * size
+        return base, size
+
     def chunk(base, size, index):
         return pl.ds(pl.multiple_of(base + index * size, LANE), size)
 
-    def along_y(p, k):
-        to = lax.rem(y + k, ny)
+    def scatter(p, level, k):
+        places, place, device = axes(p)[level]
+        base, size = span_of(p, level)
+        to = lax.rem(place + k, places)
+        size = size // places
         return pltpu.make_async_remote_copy(
-            src_ref=both.at[mp, :, chunk(p * pw, yw, to)],
-            dst_ref=ybuf.at[p, k - 1],
-            send_sem=ysend.at[p, k - 1],
-            recv_sem=yrecv.at[p, k - 1],
-            device_id={"dp": z * ny + to},
+            src_ref=both.at[mp, :, chunk(base, size, to)],
+            dst_ref=slots.at[p, level, k - 1, :, pl.ds(0, size)],
+            send_sem=rsend.at[p, level, k - 1],
+            recv_sem=rrecv.at[p, level, k - 1],
+            device_id={"dp": device(to)},
             device_id_type=MESH,
         )
 
-    def along_z(p, k):
-        to = lax.rem(z + k, nz)
-        return pltpu.make_async_remote_copy(
-            src_ref=both.at[mp, :, chunk(p * pw + y * yw, zw, to)],
-            dst_ref=zbuf.at[p, k - 1],
-            send_sem=zsend.at[p, k - 1],
-            recv_sem=zrecv.at[p, k - 1],
-            device_id={"dp": to * ny + y},
-            device_id_type=MESH,
-        )
-
-    def gather_z(p, k):
-        to = lax.rem(z + k, nz)
-        at = chunk(p * pw + y * yw, zw, z)
+    def gather(p, level, k):
+        places, place, device = axes(p)[level]
+        base, size = span_of(p, level)
+        to = lax.rem(place + k, places)
+        size = size // places
+        at = chunk(base, size, place)
         return pltpu.make_async_remote_copy(
             src_ref=res.at[:, at],
             dst_ref=res.at[:, at],
-            send_sem=azsend.at[p, k - 1],
-            recv_sem=azrecv.at[p, k - 1],
-            device_id={"dp": to * ny + y},
+            send_sem=gsend.at[p, level, k - 1],
+            recv_sem=grecv.at[p, level, k - 1],
+            device_id={"dp": device(to)},
             device_id_type=MESH,
         )
 
-    def gather_y(p, k):
-        to = lax.rem(y + k, ny)
-        at = chunk(p * pw, yw, y)
-        return pltpu.make_async_remote_copy(
-            src_ref=res.at[:, at],
-            dst_ref=res.at[:, at],
-            send_sem=aysend.at[p, k - 1],
-            recv_sem=ayrecv.at[p, k - 1],
-            device_id={"dp": z * ny + to},
-            device_id_type=MESH,
-        )
-
-    def start(copy):
-        copy.start()
-        waits.append(copy)
+    def others(p, level):
+        return range(1, axes(p)[level][0])
+
+    def reduce(p, level):
+        base, size = span_of(p, level + 1)
+        at = chunk(base, size, 0)
+        acc = both[mp, :, at]
+        for k in others(p, level):
+            scatter(p, level, k).wait_recv()
+            acc = acc + slots[p, level, k - 1, :, pl.ds(0, size)]
+        return at, acc
 
     for p in range(pieces):
         compute_piece(p, other)
@@ -353,34 +370,27 @@
         to_sibling(p).wait_recv()
         at = pl.ds(p * pw, pw)
         both[mp, :, at] = both[mp, :, at] + sib[:, at]
-        for k in range(1, ny):
-            start(along_y(p, k))
+        for k in others(p, 0):
+            start(scatter(p, 0, k))
+    order = list(range(first_z, pieces)) + list(range(first_z))
+    for p in order:
+        at, acc = reduce(p, 0)
+        both[mp, :, at] = acc
+        for k in others(p, 1):
+            start(scatter(p, 1, k))
+    for p in order[::-1]:
+        at, acc = reduce(p, 1)
+        res[:, at] = acc
+        for k in others(p, 1):
+            start(gather(p, 1, k))
+    for p in order[::-1]:
+        for k in others(p, 1):
+            gather(p, 1, k).wait_recv()
+        for k in others(p, 0):
+            start(gather(p, 0, k))
     for p in range(pieces):
-        at = chunk(p * pw, yw, y)
-        acc = both[mp, :, at]
-        for k in range(1, ny):
-            along_y(p, k).wait_recv()
-            acc = acc + ybuf[p, k - 1]
-        both[mp, :, at] = acc
-        for k in range(1, nz):
-            start(along_z(p, k))
-    for p in range(pieces):
-        at = chunk(p * pw + y * yw, zw, z)
-        acc = both[mp, :, at]
-        for k in range(1, nz):
-            along_z(p, k).wait_recv()
-            acc = acc + zbuf[p, k - 1]
-        res[:, at] = acc
-        for k in range(1, nz):
-            start(gather_z(p, k))
-    for p in range(pieces):
-        for k in range(1, nz):
-            gather_z(p, k).wait_recv()
-        for k in range(1, ny):
-            start(gather_y(p, k))
-    for p in range(pieces):
-        for k in range(1, ny):
-            gather_y(p, k).wait_recv()
+        for k in others(p, 0):
+            gather(p, 0, k).wait_recv()
         lo, hi = p * pw, min((p + 1) * pw, hu)
         if lo < hi:
             gup_ref[:, pl.ds(lo, hi - lo)] = res[:, pl.ds(lo, hi - lo)]
@@ -407,10 +417,8 @@
     rank = adapter_down_factor.shape[0]
     total = positives.shape[0]
     pieces, cols, ny, nz = plan(n, width, units)
-    yw = cols // pieces // ny
-    zw = yw // nz
+    least, most = max(min(ny, nz), 1), max(ny, nz, 2)
     chunks = 7
-    sy, sz = max(ny - 1, 1), max(nz - 1, 1)
     dma = pltpu.SemaphoreType.DMA
     vmem = pl.BlockSpec(memory_space=pltpu.VMEM)
     smem = pl.BlockSpec(memory_space=pltpu.SMEM)
@@ -422,38 +430,37 @@
             jax.ShapeDtypeStruct((rank, width // 2), F32),
             jax.ShapeDtypeStruct((1,), F32),
         ),
-        in_specs=[hbm, hbm, smem, vmem, hbm, vmem, vmem],
+        in_specs=[hbm] * 7,
         out_specs=(vmem, vmem, smem),
         scratch_shapes=[
             pltpu.VMEM((span, width), BF16),
             pltpu.VMEM((span, units), BF16),
             pltpu.VMEM((rank, units), BF16),
+            pltpu.SMEM((1,), jnp.int32),
+            pltpu.VMEM((1, total), jnp.int32),
+            pltpu.VMEM((rank, width), BF16),
+            pltpu.VMEM((1, width), F32),
             pltpu.VMEM((span, width), F32),
             pltpu.VMEM((width // LANE, LANE), F32),
             pltpu.VMEM((total * (width // LANE), LANE), F32),
             pltpu.VMEM((2, rank, cols), F32),
             pltpu.VMEM((rank, cols), F32),
-            pltpu.VMEM((pieces, sy, rank, yw), F32),
-            pltpu.VMEM((pieces, sz, rank, zw), F32),
+            pltpu.VMEM((pieces, 2, most - 1, rank, cols // pieces // least), F32),
             pltpu.VMEM((rank, cols), F32),
-            dma((2, chunks + 1)),
+            dma((3, max(chunks, 5))),
             dma((n,)),
             dma((n,)),
             dma((n,)),
             dma((n,)),
             dma((pieces,)),
             dma((pieces,)),
-            dma((pieces, sy)),
-            dma((pieces, sy)),
-            dma((pieces, sz)),
-            dma((pieces, sz)),
-            dma((pieces, sz)),
-            dma((pieces, sz)),
-            dma((pieces, sy)),
-            dma((pieces, sy)),
+            dma((pieces, 2, most - 1)),
+            dma((pieces, 2, most - 1)),
+            dma((pieces, 2, most - 1)),
+            dma((pieces, 2, most - 1)),
         ],
         compiler_params=pltpu.CompilerParams(
-            collective_id=0, has_side_effects=True, vmem_limit_bytes=40 * 2**20
+            collective_id=0, has_side_effects=True, vmem_limit_bytes=60 * 2**20
         ),
     )(
         frozen_state,

time: 52.9 us -> 46.6 us (0.88)
  local copies, waits for them, and re-layouts: 7.97 us -> 3.38 us
  Pallas kernels: 41.4 us -> 39.9 us
    unnamed x14 -> x2, local copies, waits for them, and re-layouts: 7.97 us -> 3.38 us
    pallas_call x1, Pallas kernels: 41.4 us -> 39.9 us  [body(): pl.pallas_call(functools.partial(kernel, n, chunks), out_shape=(jax.Shape...]
where the time goes in v2:
time: 46.6 us; the launch traced here: 46.4 us
  Pallas kernels  39.9 us (86%)
  local copies, waits for them, and re-layouts  3.38 us (7%)
  between operations  3.09 us (7%)
    pallas_call x1, Pallas kernels, body(): pl.pallas_call(functools.partial(kernel, n, chunks), out_shape=(jax.Shape...  39.9 us
    unnamed x2, local copies, waits for them, and re-layouts  3.38 us

profile of v2, /device:TPU:0, one launch (start us, length us, event | category | flops | bytes accessed | tf_op | source)
XLA Modules:
  0.0 46.4 jit_solution(13776458243939074714)
XLA Ops:
  1.3 39.9 %shard_map.94 = (f32[16,7168]{1,0:T(8,128)}, f32[16,2048]{1,0:T(8,128)}, f32[1]{0:T(128)}) custom-call(bf16[1,128,4096]{2,1,0:T(8,128)(2,1)} %frozen_hbm.1, bf16[1,128,14336]{2,1,0:T(8,128)(2,1)} %hidden_hbm.1, s32[1]{0:T(128)S(6)} %copy.13.lengths_hbm, s32[1,16]{1,0:T(1,128)} %bitcast.3, bf16[16,14336]{1,0:T(8,128)(2,1)} %down_hbm.1, ...), custom_call_target="tpu_custom_call" | custom-call | tf_op jit(solution)/shard_map/pallas_call | solution.py:426
  41.2 1.8 %copy.14 = f32[16,7168]{1,0:T(8,128)} copy(f32[16,7168]{1,0:T(8,128)} %get-tuple-element.6) | data formatting | bytes 917504
  43.0 1.6 %copy.15 = f32[16,2048]{1,0:T(8,128)} copy(f32[16,2048]{1,0:T(8,128)} %get-tuple-element.7) | data formatting | bytes 262144

commit v3 on v2

--- a/solution.py
+++ b/solution.py
@@ -18,12 +18,26 @@
 
 
 def plan(n, width, hidden):
-    blocks = (width + hidden) // 2 // LANE
-    pieces = 3 if blocks % (3 * n) == 0 else 1
-    unit = n * pieces
-    padded = (blocks + unit - 1) // unit * unit
+    per = -(-(width + hidden) // 2 // LANE // n)
+    if per >= 9:
+        first, second = 3 * per // 9, 3 * per // 9
+        parts = (first, second, per - first - second)
+    else:
+        parts = (per,)
     ny = max(d for d in range(1, int(math.isqrt(n)) + 1) if n % d == 0)
-    return pieces, padded * LANE, ny, n // ny
+    return tuple(w * n * LANE for w in parts), ny, n // ny
+
+
+STEPS = {
+    1: (("sib", 0), ("s0", 0), ("r0", 0), ("r1", 0), ("g1", 0), ("out", 0)),
+    3: (
+        ("sib", 0), ("s0", 0), ("sib", 1), ("s0", 1), ("sib", 2), ("s0", 2),
+        ("r0", 1), ("r0", 0), ("r0", 2),
+        ("r1", 0), ("r1", 1), ("r1", 2),
+        ("g1", 1), ("g1", 0), ("g1", 2),
+        ("out", 1), ("out", 0), ("out", 2),
+    ),
+}
 
 
 def nt_dot(a, b, precision=None):
@@ -42,8 +56,8 @@
     down_hbm,
     up_hbm,
     gain_hbm,
-    gdown_ref,
-    gup_ref,
+    gdown_hbm,
+    gup_hbm,
     loss_ref,
     frozen,
     hidden,
@@ -70,14 +84,16 @@
     rrecv,
     gsend,
     grecv,
+    osem,
 ):
     span, width = frozen.shape
     units = hidden.shape[1]
     rank = up_ref.shape[0]
     total = 2 * n
     rows = width // LANE
-    pieces, cols, ny, nz = plan(n, width, units)
-    pw = cols // pieces
+    widths, ny, nz = plan(n, width, units)
+    pieces = len(widths)
+    bases = [sum(widths[:p]) for p in range(pieces)]
     first_z = 1 if pieces > 1 else 0
     hu, hd = width // 2, units // 2
     dp = lax.axis_index("dp")
@@ -274,7 +290,8 @@
     dlow_t = dlow.astype(BF16).astype(F32).T.astype(BF16)
 
     def compute_piece(p, half):
-        lo, hi = max(p * pw, hu), min((p + 1) * pw, hu + hd)
+        end = bases[p] + widths[p]
+        lo, hi = max(bases[p], hu), min(end, hu + hd)
         while lo < hi:
             w = min(1024, hi - lo)
             at = pl.ds(pl.multiple_of(half * hd + (lo - hu), LANE), w)
@@ -282,11 +299,9 @@
                 dlow_t, hidden[:, at], preferred_element_type=F32
             )
             lo += w
-        lo = max(p * pw, hu + hd)
-        if lo < (p + 1) * pw:
-            both[half, :, pl.ds(lo, (p + 1) * pw - lo)] = jnp.zeros(
-                (rank, (p + 1) * pw - lo), F32
-            )
+        lo = max(bases[p], hu + hd)
+        if lo < end:
+            both[half, :, pl.ds(lo, end - lo)] = jnp.zeros((rank, end - lo), F32)
 
     waits = []
 
@@ -295,7 +310,7 @@
         waits.append(copy)
 
     def to_sibling(p):
-        at = pl.ds(p * pw, pw)
+        at = pl.ds(bases[p], widths[p])
         return pltpu.make_async_remote_copy(
             src_ref=both.at[other, :, at],
             dst_ref=sib.at[:, at],
@@ -312,7 +327,7 @@
         return (along_z, along_y) if p < first_z else (along_y, along_z)
 
     def span_of(p, level):
-        base, size = p * pw, pw
+        base, size = bases[p], widths[p]
         for places, place, _ in axes(p)[:level]:
             size = size // places
             base = base + place * size
@@ -362,43 +377,58 @@
             acc = acc + slots[p, level, k - 1, :, pl.ds(0, size)]
         return at, acc
 
+    out_copies = []
+
+    def write_out(p):
+        end = bases[p] + widths[p]
+        for c, (ref, first, last) in enumerate(
+            ((gup_hbm, 0, hu), (gdown_hbm, hu, hu + hd))
+        ):
+            lo, hi = max(bases[p], first), min(end, last)
+            if lo < hi:
+                copy = pltpu.make_async_copy(
+                    res.at[:, pl.ds(lo, hi - lo)],
+                    ref.at[:, pl.ds(lo - first, hi - lo)],
+                    osem.at[p, c],
+                )
+                copy.start()
+                out_copies.append(copy)
+
     for p in range(pieces):
         compute_piece(p, other)
         start(to_sibling(p))
-    for p in range(pieces):
-        compute_piece(p, mp)
-        to_sibling(p).wait_recv()
-        at = pl.ds(p * pw, pw)
-        both[mp, :, at] = both[mp, :, at] + sib[:, at]
-        for k in others(p, 0):
-            start(scatter(p, 0, k))
-    order = list(range(first_z, pieces)) + list(range(first_z))
-    for p in order:
-        at, acc = reduce(p, 0)
-        both[mp, :, at] = acc
-        for k in others(p, 1):
-            start(scatter(p, 1, k))
-    for p in order[::-1]:
-        at, acc = reduce(p, 1)
-        res[:, at] = acc
-        for k in others(p, 1):
-            start(gather(p, 1, k))
-    for p in order[::-1]:
-        for k in others(p, 1):
-            gather(p, 1, k).wait_recv()
-        for k in others(p, 0):
-            start(gather(p, 0, k))
-    for p in range(pieces):
-        for k in others(p, 0):
-            gather(p, 0, k).wait_recv()
-        lo, hi = p * pw, min((p + 1) * pw, hu)
-        if lo < hi:
-            gup_ref[:, pl.ds(lo, hi - lo)] = res[:, pl.ds(lo, hi - lo)]
-        lo, hi = max(p * pw, hu), min((p + 1) * pw, hu + hd)
-        if lo < hi:
-            gdown_ref[:, pl.ds(lo - hu, hi - lo)] = res[:, pl.ds(lo, hi - lo)]
+    for step, p in STEPS[pieces]:
+        if step == "sib":
+            compute_piece(p, mp)
+            to_sibling(p).wait_recv()
+            at = pl.ds(bases[p], widths[p])
+            both[mp, :, at] = both[mp, :, at] + sib[:, at]
+        elif step == "s0":
+            for k in others(p, 0):
+                start(scatter(p, 0, k))
+        elif step == "r0":
+            at, acc = reduce(p, 0)
+            both[mp, :, at] = acc
+            for k in others(p, 1):
+                start(scatter(p, 1, k))
+        elif step == "r1":
+            at, acc = reduce(p, 1)
+            res[:, at] = acc
+            for k in others(p, 1):
+                start(gather(p, 1, k))
+        elif step == "g1":
+            for k in others(p, 1):
+                gather(p, 1, k).wait_recv()
+            for k in others(p, 0):
+                start(gather(p, 0, k))
+        else:
+            for k in others(p, 0):
+                gather(p, 0, k).wait_recv()
+            write_out(p)
     for copy in waits:
         copy.wait_send()
+    for copy in out_copies:
+        copy.wait()
 
 
 def body(
@@ -416,11 +446,11 @@
     units = gated_hidden.shape[2]
     rank = adapter_down_factor.shape[0]
     total = positives.shape[0]
-    pieces, cols, ny, nz = plan(n, width, units)
+    widths, ny, nz = plan(n, width, units)
+    pieces, cols = len(widths), sum(widths)
     least, most = max(min(ny, nz), 1), max(ny, nz, 2)
     chunks = 7
     dma = pltpu.SemaphoreType.DMA
-    vmem = pl.BlockSpec(memory_space=pltpu.VMEM)
     smem = pl.BlockSpec(memory_space=pltpu.SMEM)
     hbm = pl.BlockSpec(memory_space=pl.ANY)
     grad_down, grad_up, mean_loss = pl.pallas_call(
@@ -431,7 +461,7 @@
             jax.ShapeDtypeStruct((1,), F32),
         ),
         in_specs=[hbm] * 7,
-        out_specs=(vmem, vmem, smem),
+        out_specs=(hbm, hbm, smem),
         scratch_shapes=[
             pltpu.VMEM((span, width), BF16),
             pltpu.VMEM((span, units), BF16),
@@ -445,7 +475,7 @@
             pltpu.VMEM((total * (width // LANE), LANE), F32),
             pltpu.VMEM((2, rank, cols), F32),
             pltpu.VMEM((rank, cols), F32),
-            pltpu.VMEM((pieces, 2, most - 1, rank, cols // pieces // least), F32),
+            pltpu.VMEM((pieces, 2, most - 1, rank, max(widths) // least), F32),
             pltpu.VMEM((rank, cols), F32),
             dma((3, max(chunks, 5))),
             dma((n,)),
@@ -458,6 +488,7 @@
             dma((pieces, 2, most - 1)),
             dma((pieces, 2, most - 1)),
             dma((pieces, 2, most - 1)),
+            dma((pieces, 2)),
         ],
         compiler_params=pltpu.CompilerParams(
             collective_id=0, has_side_effects=True, vmem_limit_bytes=60 * 2**20

time: 46.6 us -> 45.3 us (0.972)
  Pallas kernels: 39.9 us -> 38.6 us
    pallas_call x1, Pallas kernels: 39.9 us -> 38.6 us  [body(): pl.pallas_call(functools.partial(kernel, n, chunks), out_shape=(jax.Shape...]
where the time goes in v3:
time: 45.3 us; the launch traced here: 45.1 us
  Pallas kernels  38.6 us (85%)
  local copies, waits for them, and re-layouts  3.38 us (7%)
  between operations  3.09 us (7%)
    pallas_call x1, Pallas kernels, body(): pl.pallas_call(functools.partial(kernel, n, chunks), out_shape=(jax.Shape...  38.6 us
    unnamed x2, local copies, waits for them, and re-layouts  3.38 us

profile of v3, /device:TPU:0, one launch (start us, length us, event | category | flops | bytes accessed | tf_op | source)
XLA Modules:
  0.0 45.1 jit_solution(8086837181582921658)
XLA Ops:
  1.3 38.6 %shard_map.94 = (f32[16,7168]{1,0:T(8,128)}, f32[16,2048]{1,0:T(8,128)}, f32[1]{0:T(128)}) custom-call(bf16[1,128,4096]{2,1,0:T(8,128)(2,1)} %frozen_hbm.1, bf16[1,128,14336]{2,1,0:T(8,128)(2,1)} %hidden_hbm.1, s32[1]{0:T(128)S(6)} %copy.13.lengths_hbm, s32[1,16]{1,0:T(1,128)} %bitcast.3, bf16[16,14336]{1,0:T(8,128)(2,1)} %down_hbm.1, ...), custom_call_target="tpu_custom_call" | custom-call | tf_op jit(solution)/shard_map/pallas_call | solution.py:456
  39.9 1.8 %copy.14 = f32[16,7168]{1,0:T(8,128)} copy(f32[16,7168]{1,0:T(8,128)} %get-tuple-element.6) | data formatting | bytes 917504
  41.7 1.6 %copy.15 = f32[16,2048]{1,0:T(8,128)} copy(f32[16,2048]{1,0:T(8,128)} %get-tuple-element.7) | data formatting | bytes 262144
